TPU v7x, 32 devices: a whole 2x2x4 slice. The times are simulated.
32 devices in a mesh: dp: 4 (over x, core), ctx: 8 (over z, y).
Axes of the slice: x: 2, y: 2, z: 4, core: 2. Of those that a mesh axis runs over, the one named last changes fastest.
Arguments:
- query: bfloat16 [4, 1024, 8192], P('dp', 'ctx'), may hold values from -10 to 10
- key: bfloat16 [4, 1024, 1024], P('dp', 'ctx'), may hold values from -16 to 16
- value: bfloat16 [4, 1024, 1024], P('dp', 'ctx'), may hold values from -6 to 6
- out_grad: bfloat16 [4, 1024, 8192], P('dp', 'ctx'), may hold values from -6 to 6
- loss_mask: int32 [4, 1024], P('dp', 'ctx'), may hold values from 0 to 1, as said below
Outputs:
- attended: bfloat16 [4, 1024, 8192], P('dp', 'ctx')
- query_grad: bfloat16 [4, 1024, 8192], P('dp', 'ctx')
- key_grad: bfloat16 [4, 1024, 1024], P('dp', 'ctx')
- value_grad: bfloat16 [4, 1024, 1024], P('dp', 'ctx')
Inputs may be any that keep to these rules, and one draw needn't show every extreme that they name: `loss_mask`: the last position of every sequence is 1.
All inputs are finite; a program needn't handle non-finite values.
Results may differ from a plain program's by a relative error of at most 0.015.
Values may be sent and summed in bfloat16 or wider, within the bound.
A program may use at most 128 MiB of HBM per device.

v0:
```python
import math

import jax
import jax.numpy as jnp
from jax import lax
from jax.sharding import PartitionSpec as P

QUERY_HEADS = 64
KEY_VALUE_HEADS = 8
HEAD_SIZE = 128
BLOCK = 512


def swapped(block, axis, distance):
    count = lax.axis_size(axis)
    route = []
    for low in range(count):
        high = low | 1 << distance
        if high != low and high < count:
            route += [(low, high), (high, low)]
    return lax.ppermute(block, axis, route)


def mirror_rows(block, shard_pieces):
    length = block.shape[0]
    halves = block.reshape((shard_pieces, 2, length // (2 * shard_pieces)) + block.shape[1:])
    return jnp.stack([halves[:, 0], jnp.roll(halves[:, 1], shard_pieces // 2, axis=0)], 1).reshape(
        block.shape
    )


def tile_scores(query_tile, key_tile, row_start, col_start):
    products = jnp.einsum(
        "qhe,ke->hqk", query_tile, key_tile, preferred_element_type=jnp.float32
    ) * (1.0 / math.sqrt(HEAD_SIZE))
    row_pos = row_start + jnp.arange(query_tile.shape[0])
    col_pos = col_start + jnp.arange(key_tile.shape[0])
    return jnp.where(row_pos[:, None] >= col_pos[None, :], products, -1e30)


def attend_heads(pieces, keys, values, shard_pieces):
    query_rows, gradient_rows = pieces
    query_rows = mirror_rows(query_rows, shard_pieces)
    gradient_rows = mirror_rows(gradient_rows, shard_pieces)
    query_rows = query_rows[:, 0]
    gradient_rows = gradient_rows[:, 0]
    length, heads, width = query_rows.shape
    blocks = length // BLOCK
    zero_tile = jnp.zeros((BLOCK, heads, width), jnp.float32)

    def log_norm(row_block, norms):
        start = row_block * BLOCK
        query_tile = lax.dynamic_slice_in_dim(query_rows, start, BLOCK, 0)

        def absorb(col_block, carry):
            peak, mass = carry
            key_tile = lax.dynamic_slice_in_dim(keys, col_block * BLOCK, BLOCK, 0)
            scores = tile_scores(query_tile, key_tile, start, col_block * BLOCK)
            new_peak = jnp.maximum(peak, jnp.max(scores, axis=-1))
            mass = mass * jnp.exp(peak - new_peak) + jnp.sum(
                jnp.exp(scores - new_peak[:, :, None]), axis=-1
            )
            return (new_peak, mass)

        first = (
            jnp.full((heads, BLOCK), -1e30, jnp.float32),
            jnp.zeros((heads, BLOCK), jnp.float32),
        )
        peak, mass = lax.fori_loop(0, row_block + 1, absorb, first)
        return lax.dynamic_update_slice_in_dim(norms, peak + jnp.log(mass), start, 1)

    norms = lax.fori_loop(0, blocks, log_norm, jnp.zeros((heads, length), jnp.float32))

    def forward_block(row_block, carry):
        outputs, deltas = carry
        start = row_block * BLOCK
        query_tile = lax.dynamic_slice_in_dim(query_rows, start, BLOCK, 0)
        grad_tile = lax.dynamic_slice_in_dim(gradient_rows, start, BLOCK, 0)
        norm_tile = lax.dynamic_slice_in_dim(norms, start, BLOCK, 1)

        def gather_values(col_block, accum):
            col_start = col_block * BLOCK
            key_tile = lax.dynamic_slice_in_dim(keys, col_start, BLOCK, 0)
            value_tile = lax.dynamic_slice_in_dim(values, col_start, BLOCK, 0)
            weights = jnp.exp(
                tile_scores(query_tile, key_tile, start, col_start) - norm_tile[:, :, None]
            ).astype(jnp.bfloat16)
            return accum + jnp.einsum(
                "hqk,ke->qhe", weights, value_tile, preferred_element_type=jnp.float32
            )

        accum = lax.fori_loop(0, row_block + 1, gather_values, zero_tile)
        out_tile = accum.astype(jnp.bfloat16)
        delta_tile = jnp.einsum(
            "qhe,qhe->hq", grad_tile, out_tile, preferred_element_type=jnp.float32
        )
        outputs = lax.dynamic_update_slice_in_dim(outputs, out_tile, start, 0)
        deltas = lax.dynamic_update_slice_in_dim(deltas, delta_tile, start, 1)
        return (outputs, deltas)

    outputs, deltas = lax.fori_loop(
        0,
        blocks,
        forward_block,
        (jnp.zeros((length, heads, width), jnp.bfloat16), jnp.zeros((heads, length), jnp.float32)),
    )

    def backward_block(col_block, carry):
        query_grad, key_grad, value_grad = carry
        col_start = col_block * BLOCK
        key_tile = lax.dynamic_slice_in_dim(keys, col_start, BLOCK, 0)
        value_tile = lax.dynamic_slice_in_dim(values, col_start, BLOCK, 0)

        def visit(row_block, inner):
            query_grad, key_accum, value_accum = inner
            start = row_block * BLOCK
            query_tile = lax.dynamic_slice_in_dim(query_rows, start, BLOCK, 0)
            grad_tile = lax.dynamic_slice_in_dim(gradient_rows, start, BLOCK, 0)
            norm_tile = lax.dynamic_slice_in_dim(norms, start, BLOCK, 1)
            delta_tile = lax.dynamic_slice_in_dim(deltas, start, BLOCK, 1)
            probs = jnp.exp(
                tile_scores(query_tile, key_tile, start, col_start) - norm_tile[:, :, None]
            )
            weights = probs.astype(jnp.bfloat16)
            value_accum = value_accum + jnp.einsum(
                "hqk,qhe->khe", weights, grad_tile, preferred_element_type=jnp.float32
            )
            dots = jnp.einsum(
                "qhe,ke->hqk", grad_tile, value_tile, preferred_element_type=jnp.float32
            )
            slopes = (probs * (dots - delta_tile[:, :, None])).astype(jnp.bfloat16)
            key_accum = key_accum + jnp.einsum(
                "hqk,qhe->khe", slopes, query_tile, preferred_element_type=jnp.float32
            )
            previous = lax.dynamic_slice_in_dim(query_grad, start, BLOCK, 0)
            update = previous + jnp.einsum(
                "hqk,ke->qhe", slopes, key_tile, preferred_element_type=jnp.float32
            )
            query_grad = lax.dynamic_update_slice_in_dim(query_grad, update, start, 0)
            return (query_grad, key_accum, value_accum)

        query_grad, key_accum, value_accum = lax.fori_loop(
            col_block, blocks, visit, (query_grad, zero_tile, zero_tile)
        )
        key_grad = lax.dynamic_update_slice_in_dim(key_grad, key_accum, col_start, 0)
        value_grad = lax.dynamic_update_slice_in_dim(value_grad, value_accum, col_start, 0)
        return (query_grad, key_grad, value_grad)

    zero_full = jnp.zeros((length, heads, width), jnp.float32)
    query_grad, key_grad, value_grad = lax.fori_loop(
        0, blocks, backward_block, (zero_full, zero_full, zero_full)
    )
    query_out = (query_grad * (1.0 / math.sqrt(HEAD_SIZE))).astype(jnp.bfloat16)
    return (outputs[:, None], query_out[:, None], key_grad[:, None], value_grad[:, None])


def body(query, key, value, out_grad, loss_mask):
    shard_pieces = lax.axis_size("ctx")
    top_bit = shard_pieces.bit_length() - 2
    resident_rows = query.shape[1]
    half_rows = resident_rows // 2
    local_heads = QUERY_HEADS // shard_pieces
    replica_copies = shard_pieces // KEY_VALUE_HEADS
    all_tokens = query.shape[0] * resident_rows * shard_pieces * lax.axis_size("dp")
    loss_count = lax.psum(jnp.sum(loss_mask).astype(jnp.float32), ("dp", "ctx"))
    token_weight = loss_mask[0].astype(jnp.float32) * (all_tokens / loss_count)
    grads_in = (out_grad[0].astype(jnp.float32) * token_weight[:, None]).astype(jnp.bfloat16)
    queries = query[0]
    key_value = jnp.stack(
        [
            key[0].reshape(resident_rows, KEY_VALUE_HEADS, HEAD_SIZE),
            value[0].reshape(resident_rows, KEY_VALUE_HEADS, HEAD_SIZE),
        ],
        axis=2,
    )
    kv_send = jnp.repeat(key_value, replica_copies, axis=1).reshape(
        resident_rows, shard_pieces, 2 * HEAD_SIZE
    )
    later_query, later_grad, later_kv = swapped(
        (queries[half_rows:], grads_in[half_rows:], kv_send[half_rows:]), "ctx", top_bit
    )
    queries = jnp.concatenate([queries[:half_rows], later_query], 0)
    grads_in = jnp.concatenate([grads_in[:half_rows], later_grad], 0)
    kv_send = jnp.concatenate([kv_send[:half_rows], later_kv], 0)
    kv_rows = lax.all_to_all(kv_send, "ctx", split_axis=1, concat_axis=0, tiled=True)[:, 0]
    kv_rows = mirror_rows(kv_rows, shard_pieces)
    keys = kv_rows[:, :HEAD_SIZE]
    values = kv_rows[:, HEAD_SIZE:]
    query_split = queries.reshape(resident_rows, shard_pieces, local_heads, HEAD_SIZE)
    grad_split = grads_in.reshape(resident_rows, shard_pieces, local_heads, HEAD_SIZE)
    outputs, query_grads, key_parts, value_parts = attend_heads(
        (
            lax.all_to_all(query_split, "ctx", split_axis=1, concat_axis=0, tiled=True),
            lax.all_to_all(grad_split, "ctx", split_axis=1, concat_axis=0, tiled=True),
        ),
        keys,
        values,
        shard_pieces,
    )
    key_sum = jnp.sum(key_parts[:, 0], axis=1)
    value_sum = jnp.sum(value_parts[:, 0], axis=1)
    outputs = mirror_rows(outputs, shard_pieces)
    query_grads = mirror_rows(query_grads, shard_pieces)
    outputs, query_grads = (
        lax.all_to_all(outputs, "ctx", split_axis=0, concat_axis=1, tiled=True),
        lax.all_to_all(query_grads, "ctx", split_axis=0, concat_axis=1, tiled=True),
    )
    attended_rows = outputs.reshape(resident_rows, QUERY_HEADS * HEAD_SIZE)
    query_rows = query_grads.reshape(resident_rows, QUERY_HEADS * HEAD_SIZE)
    grad_send = jnp.stack([key_sum, value_sum], 1).reshape(key_sum.shape[0], 1, 2 * HEAD_SIZE)
    grad_send = mirror_rows(grad_send, shard_pieces)
    gradient_rows = (
        lax.all_to_all(
            grad_send.astype(jnp.bfloat16), "ctx", split_axis=0, concat_axis=1, tiled=True
        )
        .astype(grad_send.dtype)
        .reshape(resident_rows, KEY_VALUE_HEADS, replica_copies, 2, HEAD_SIZE)
        .sum(axis=2)
    )
    key_rows = (
        (gradient_rows[:, :, 0] * (1.0 / math.sqrt(HEAD_SIZE)))
        .reshape(resident_rows, KEY_VALUE_HEADS * HEAD_SIZE)
        .astype(jnp.bfloat16)
    )
    value_matrix_rows = (
        gradient_rows[:, :, 1]
        .reshape(resident_rows, KEY_VALUE_HEADS * HEAD_SIZE)
        .astype(jnp.bfloat16)
    )
    later_out, later_qgrad, later_kgrad, later_vgrad = swapped(
        (
            attended_rows[half_rows:],
            query_rows[half_rows:],
            key_rows[half_rows:],
            value_matrix_rows[half_rows:],
        ),
        "ctx",
        top_bit,
    )
    attended_rows = jnp.concatenate([attended_rows[:half_rows], later_out], 0)
    query_rows = jnp.concatenate([query_rows[:half_rows], later_qgrad], 0)
    key_rows = jnp.concatenate([key_rows[:half_rows], later_kgrad], 0)
    value_matrix_rows = jnp.concatenate([value_matrix_rows[:half_rows], later_vgrad], 0)
    return (attended_rows[None], query_rows[None], key_rows[None], value_matrix_rows[None])


def solution(mesh):
    placed = (
        P("dp", "ctx", None),
        P("dp", "ctx", None),
        P("dp", "ctx", None),
        P("dp", "ctx", None),
        P("dp", "ctx"),
    )
    return jax.shard_map(
        body,
        mesh=mesh,
        in_specs=placed,
        out_specs=(
            P("dp", "ctx", None),
            P("dp", "ctx", None),
            P("dp", "ctx", None),
            P("dp", "ctx", None),
        ),
        check_vma=False,
    )
```

profile of v0, /device:TPU:0, one launch (start us, length us, event | category | flops | bytes accessed | tf_op | source)
XLA Modules:
  0.0 656.1 jit_solution(2882076997061066133)
XLA Ops:
  2.6 42.0 %psum.7 = f32[]{:T(128)} all-reduce(f32[]{:T(128)S(6)} %convert_element_type.71), channel_id=1, replica_groups=mesh['dp'=4,'ctx'=8] {'dp','ctx'}, use_global_device_ids=true, to_apply=%region_1.0 | all-reduce | flops 1 | bytes 8 | tf_op jit(solution)/shard_map/psum | solution.py:165
  56.5 55.8 %collective-permute-done.1 = bf16[64,8,256]{2,1,0:T(8,128)(2,1)S(1)} collective-permute-done((bf16[64,8,256]{2,1,0:T(8,128)(2,1)S(1)}, bf16[64,8,256]{2,1,0:T(8,128)(2,1)S(1)}, u32[]{:S(2)}, u32[]{:S(2)}) %collective-permute-start.1) | collective-permute-done | bytes 262176 | tf_op jit(solution)/shard_map/ppermute | solution.py:21
  113.3 4.3 all-to-all-start.1
  123.7 7.5 %all-to-all-done.1 = bf16[128,8,256]{2,0,1:T(8,128)(2,1)S(1)} async-done(((bf16[128,8,256]{2,0,1:T(8,128)(2,1)}), bf16[128,8,256]{2,0,1:T(8,128)(2,1)S(1)}, u32[]{:S(2)}, u32[]{:S(2)}) %all-to-all-start.1) | async-done | bytes 524320 | tf_op jit(solution)/shard_map/all_to_all | solution.py:185
  139.7 87.5 %collective-permute-done = bf16[64,8192]{1,0:T(8,128)(2,1)S(1)} collective-permute-done((bf16[64,8192]{1,0:T(8,128)(2,1)S(1)}, bf16[64,8192]{1,0:T(8,128)(2,1)S(1)}, u32[]{:S(2)}, u32[]{:S(2)}) %collective-permute-start) | collective-permute-done | bytes 1048608 | tf_op jit(solution)/shard_map/ppermute | solution.py:21
  229.4 4.5 all-to-all-start
  239.8 41.9 %all-to-all-done = bf16[128,8,8,128]{3,2,0,1:T(8,128)(2,1)} async-done(((bf16[128,8,8,128]{3,2,0,1:T(8,128)(2,1)}), bf16[128,8,8,128]{3,2,0,1:T(8,128)(2,1)}, u32[]{:S(2)}, u32[]{:S(2)}) %all-to-all-start) | async-done | bytes 2097184 | tf_op jit(solution)/shard_map/all_to_all | solution.py:193
  291.5 13.4 %while.128 = (s32[]{:T(128)}, f32[8,1024]{1,0:T(8,128)S(1)}, bf16[1024,8,128]{2,0,1:T(8,128)(2,1)}, bf16[1024,128]{1,0:T(8,128)(2,1)S(1)}, s32[]{:T(128)}, /*ind...) while((s32[]{:T(128)}, f32[8,1024]{1,0:T(8,128)S(1)}, ...), condition=%wide.region_7.8_spmd, body=%wide.region_2.7_spmd.sunk | while | flops 551826432 | bytes 21144012 | solution.py:72
  297.8 7.1 %while.133 = (s32[]{:T(128)}, f32[8,512]{1,0:T(8,128)S(1)}, f32[8,512]{1,0:T(8,128)S(1)}, s32[]{:T(128)}, s32[]{:T(128)}, /*index=5*/bf16[1024,128]{1,0:T(8,128)...) while((s32[]{:T(128)}, f32[8,512]{1,0:T(8,128)S(1)}, ...), condition=%wide.region_6.6_spmd, body=%wide.region_3.5_spmd.sunk | while | flops 551822336 | bytes 18964648 | solution.py:69
  306.5 44.5 %while.130 = (s32[]{:T(128)}, bf16[1024,8,128]{2,1,0:T(8,128)(2,1)}, f32[8,1024]{1,0:T(8,128)S(1)}, bf16[1024,8,128]{2,0,1:T(8,128)(2,1)}, f32[8,1024]{1,0:T(8,1...) while((s32[]{:T(128)}, bf16[1024,8,128]{2,1,0:T(8,128)(2,1)}, ...), condition=%wide.region_11.12_spmd, body=%wide.region_8.11_spmd.sunk | while | flops 1085535232 | bytes 27108852 | solution.py:101
  315.1 6.4 while.134
  315.3 6.2 bitcast_add_fusion.9
  334.0 12.9 %while.134 = (s32[]{:T(128)}, f32[512,8,128]{0,2,1:T(8,128)}, s32[]{:T(128)}, bf16[1024,128]{0,1:T(8,128)(2,1)}, s32[]{:T(128)}, /*index=5*/bf16[1024,128]{1,0:T...) while((s32[]{:T(128)}, f32[512,8,128]{0,2,1:T(8,128)}, ...), condition=%wide.region_10.10_spmd, body=%wide.region_9.9_spmd.sunk | while | flops 1082917888 | bytes 6055083 | solution.py:92
  334.2 6.2 bitcast_add_fusion.9
  340.6 6.2 bitcast_add_fusion.9
  358.4 57.5 %while.132 = (s32[]{:T(128)}, f32[1024,8,128]{2,0,1:T(8,128)}, f32[1024,8,128]{0,2,1:T(8,128)}, f32[1024,8,128]{0,2,1:T(8,128)}, bf16[1024,128]{1,0:T(8,128)(2,1...) while((s32[]{:T(128)}, f32[1024,8,128]{2,0,1:T(8,128)}, ...), condition=%wide.region_15.16_spmd, body=%wide.region_12.15_spmd.sunk | while | flops 2707162112 | bytes 127656656 | solution.py:150
  360.2 30.2 %while.135 = (s32[]{:T(128)}, f32[1024,8,128]{2,0,1:T(8,128)}, f32[512,8,128]{0,2,1:T(8,128)S(1)}, f32[512,8,128]{0,2,1:T(8,128)}, s32[]{:T(128)}, /*index=5*/bf...) while((s32[]{:T(128)}, f32[1024,8,128]{2,0,1:T(8,128)}, ...), condition=%wide.region_14.14_spmd, body=%wide.region_13.13_spmd.sunk | while | flops 2707162112 | bytes 114549096 | solution.py:142
  396.5 15.1 %while.135 = (s32[]{:T(128)}, f32[1024,8,128]{2,0,1:T(8,128)}, f32[512,8,128]{0,2,1:T(8,128)S(1)}, f32[512,8,128]{0,2,1:T(8,128)}, s32[]{:T(128)}, /*index=5*/bf...) while((s32[]{:T(128)}, f32[1024,8,128]{2,0,1:T(8,128)}, ...), condition=%wide.region_14.14_spmd, body=%wide.region_13.13_spmd.sunk | while | flops 2707162112 | bytes 114549096 | solution.py:142
  411.6 4.3 constant_dynamic-update-slice_fusion.11
  430.3 12.7 %all-to-all-done.5 = bf16[8,2,16384]{2,1,0:T(2,128)(2,1)S(1)} async-done(((bf16[8,2,16384]{2,1,0:T(2,128)(2,1)}), bf16[8,2,16384]{2,1,0:T(2,128)(2,1)S(1)}, u32[]{:S(2)}, u32[]{:S(2)}) %all-to-all-start.5) | async-done | bytes 524320 | tf_op jit(solution)/shard_map/all_to_all | solution.py:213
  447.7 4.9 fusion.53
  454.5 41.6 %all-to-all-done.3 = bf16[1024,1,8,128]{3,2,1,0:T(8,128)(2,1)S(1)} async-done(((bf16[1024,1,8,128]{3,2,1,0:T(8,128)(2,1)}), bf16[1024,1,8,128]{3,2,1,0:T(8,128)(2,1)S(1)}, u32[]{:S(2)}, u32[]{:S(2)}) %all-to-all-start.3) | async-done | bytes 2097184 | tf_op jit(solution)/shard_map/all_to_all | solution.py:205
  515.9 88.2 %collective-permute-done.5 = bf16[64,1024]{1,0:T(8,128)(2,1)S(1)} collective-permute-done((bf16[64,1024]{1,0:T(8,128)(2,1)S(1)}, bf16[64,1024]{1,0:T(8,128)(2,1)S(1)}, u32[]{:S(2)}, u32[]{:S(2)}) %collective-permute-start.5) | collective-permute-done | bytes 131104 | tf_op jit(solution)/shard_map/ppermute | solution.py:21
  613.1 39.9 %collective-permute-done.4 = bf16[64,8192]{1,0:T(8,128)(2,1)} collective-permute-done((bf16[64,8192]{1,0:T(8,128)(2,1)}, bf16[64,8192]{1,0:T(8,128)(2,1)}, u32[]{:S(2)}, u32[]{:S(2)}) %collective-permute-start.4) | collective-permute-done | bytes 1048608 | tf_op jit(solution)/shard_map/ppermute | solution.py:21
  (248 shorter events, 202.0 us)
Async XLA Ops:
  51.6 3.9 copy-start.14
  51.6 4.0 copy-start.15
  53.2 64.3 %collective-permute-start.2 = (bf16[64,8192]{1,0:T(8,128)(2,1)}, bf16[64,8192]{1,0:T(8,128)(2,1)}, u32[]{:S(2)}, u32[]{:S(2)}) collective-permute-start(bf16[64,8192]{1,0:T(8,128)(2,1)} %copy.96), channel_id=1, source_target_pairs={{0,4},{4,0},{1,5},{5,1},{2,6},{6,2},{3,7},{7,3},{8,12},{12,8},{9,1... | collective-permute-start | bytes 3145736 | tf_op jit(solution)/shard_map/ppermute | solution.py:21
  55.9 56.5 %collective-permute-start.1 = (bf16[64,8,256]{2,1,0:T(8,128)(2,1)S(1)}, bf16[64,8,256]{2,1,0:T(8,128)(2,1)S(1)}, u32[]{:S(2)}, u32[]{:S(2)}) collective-permute-start(bf16[64,8,256]{2,1,0:T(8,128)(2,1)S(1)} %get-tuple-element.758), channel_id=1, source_target_pairs={{0,4},{4,0},{1,5},{5,1},{2,6},{6,2},{3,7},{7,3},{8,12},{12,8},{9,1... | collective-permute-start | bytes 786440 | tf_op jit(solution)/shard_map/ppermute | solution.py:21
  113.3 17.8 %all-to-all-start.1 = ((bf16[128,8,256]{2,0,1:T(8,128)(2,1)}), bf16[128,8,256]{2,0,1:T(8,128)(2,1)S(1)}, u32[]{:S(2)}, u32[]{:S(2)}) async-start(bf16[128,8,256]{2,0,1:T(8,128)(2,1)} %copy.90), calls=%async_computation.1 | async-start | bytes 1048576 | tf_op jit(solution)/shard_map/all_to_all | solution.py:185
  131.1 98.3 %all-to-all-start.2 = ((bf16[128,8,8,128]{0,3,2,1:T(8,128)(2,1)}), bf16[128,8,8,128]{0,3,2,1:T(8,128)(2,1)S(1)}, u32[]{:S(2)}, u32[]{:S(2)}) async-start(bf16[128,8,8,128]{0,3,2,1:T(8,128)(2,1)} %bitcast.38), calls=%async_computation.2 | async-start | bytes 4194304 | tf_op jit(solution)/shard_map/all_to_all | solution.py:194
  136.5 90.8 %collective-permute-start = (bf16[64,8192]{1,0:T(8,128)(2,1)S(1)}, bf16[64,8192]{1,0:T(8,128)(2,1)S(1)}, u32[]{:S(2)}, u32[]{:S(2)}) collective-permute-start(bf16[64,8192]{1,0:T(8,128)(2,1)S(1)} %get-tuple-element.748), channel_id=1, source_target_pairs={{0,4},{4,0},{1,5},{5,1},{2,6},{6,2},{3,7},{7,3},{8,12},{12,8},{9,1... | collective-permute-start | bytes 3145736 | tf_op jit(solution)/shard_map/ppermute | solution.py:21
  229.4 52.3 %all-to-all-start = ((bf16[128,8,8,128]{3,2,0,1:T(8,128)(2,1)}), bf16[128,8,8,128]{3,2,0,1:T(8,128)(2,1)}, u32[]{:S(2)}, u32[]{:S(2)}) async-start(bf16[128,8,8,128]{3,2,0,1:T(8,128)(2,1)} %copy.86), calls=%async_computation | async-start | bytes 4194304 | tf_op jit(solution)/shard_map/all_to_all | solution.py:193
  234.2 3.7 copy-start.9
  366.1 3.1 copy-start.1
  369.2 2.7 copy-start.2
  375.6 2.7 copy-start
  381.2 3.1 copy-start.1
  384.3 2.7 copy-start.2
  402.4 3.1 copy-start.1
  405.5 2.7 copy-start.2
  422.1 6.2 copy-start.5
  424.7 18.3 %all-to-all-start.5 = ((bf16[8,2,16384]{2,1,0:T(2,128)(2,1)}), bf16[8,2,16384]{2,1,0:T(2,128)(2,1)S(1)}, u32[]{:S(2)}, u32[]{:S(2)}) async-start(bf16[8,2,16384]{2,1,0:T(2,128)(2,1)} %reshape.146), calls=%async_computation.5 | async-start | bytes 1048576 | tf_op jit(solution)/shard_map/all_to_all | solution.py:213
  443.8 52.3 %all-to-all-start.3 = ((bf16[1024,1,8,128]{3,2,1,0:T(8,128)(2,1)}), bf16[1024,1,8,128]{3,2,1,0:T(8,128)(2,1)S(1)}, u32[]{:S(2)}, u32[]{:S(2)}) async-start(bf16[1024,1,8,128]{3,2,1,0:T(8,128)(2,1)} %bitcast.298), calls=%async_computation.3 | async-start | bytes 4194304 | tf_op jit(solution)/shard_map/all_to_all | solution.py:205
  497.4 107.4 %all-to-all-start.4 = ((bf16[1024,1,8,128]{3,2,1,0:T(8,128)(2,1)}), bf16[1024,1,8,128]{3,2,1,0:T(8,128)(2,1)S(1)}, u32[]{:S(2)}, u32[]{:S(2)}) async-start(bf16[1024,1,8,128]{3,2,1,0:T(8,128)(2,1)} %bitcast.295), calls=%async_computation.4 | async-start | bytes 4194304 | tf_op jit(solution)/shard_map/all_to_all | solution.py:206
  507.7 101.9 %collective-permute-start.3 = (bf16[64,8192]{1,0:T(8,128)(2,1)}, bf16[64,8192]{1,0:T(8,128)(2,1)}, u32[]{:S(2)}, u32[]{:S(2)}) collective-permute-start(bf16[64,8192]{1,0:T(8,128)(2,1)} %slice.243), channel_id=1, source_target_pairs={{0,4},{4,0},{1,5},{5,1},{2,6},{6,2},{3,7},{7,3},{8,12},{12,8},{9,1... | collective-permute-start | bytes 3145736 | tf_op jit(solution)/shard_map/ppermute | solution.py:21
  511.7 92.3 %collective-permute-start.5 = (bf16[64,1024]{1,0:T(8,128)(2,1)S(1)}, bf16[64,1024]{1,0:T(8,128)(2,1)S(1)}, u32[]{:S(2)}, u32[]{:S(2)}) collective-permute-start(bf16[64,1024]{1,0:T(8,128)(2,1)S(1)} %bitcast.325), channel_id=1, source_target_pairs={{0,4},{4,0},{1,5},{5,1},{2,6},{6,2},{3,7},{7,3},{8,12},{12,8},{9,1... | collective-permute-start | bytes 393224 | tf_op jit(solution)/shard_map/ppermute | solution.py:21
  512.9 93.6 %collective-permute-start.6 = (bf16[64,1024]{1,0:T(8,128)(2,1)S(1)}, bf16[64,1024]{1,0:T(8,128)(2,1)S(1)}, u32[]{:S(2)}, u32[]{:S(2)}) collective-permute-start(bf16[64,1024]{1,0:T(8,128)(2,1)S(1)} %bitcast.324), channel_id=1, source_target_pairs={{0,4},{4,0},{1,5},{5,1},{2,6},{6,2},{3,7},{7,3},{8,12},{12,8},{9,1... | collective-permute-start | bytes 393224 | tf_op jit(solution)/shard_map/ppermute | solution.py:21
  606.5 46.4 %collective-permute-start.4 = (bf16[64,8192]{1,0:T(8,128)(2,1)}, bf16[64,8192]{1,0:T(8,128)(2,1)}, u32[]{:S(2)}, u32[]{:S(2)}) collective-permute-start(bf16[64,8192]{1,0:T(8,128)(2,1)} %slice.252), channel_id=1, source_target_pairs={{0,4},{4,0},{1,5},{5,1},{2,6},{6,2},{3,7},{7,3},{8,12},{12,8},{9,1... | collective-permute-start | bytes 3145736 | tf_op jit(solution)/shard_map/ppermute | solution.py:21
  (15 other events, 30.9 us)
where the time goes:
time: 663 us; the launch traced here: 656 us
  waiting for transfers between devices  375 us (57%)
  local copies, waits for them, and re-layouts  93.9 us (14%)
  matrix products  61.4 us (9%)
  other arithmetic  44 us (7%)
  blocking collectives  42 us (6%)
  starting transfers between devices  35.6 us (5%)
    ppermute x7, waiting for transfers between devices, swapped(): return lax.ppermute(block, axis, route)  271 us
    psum x1, blocking collectives, body(): loss_count = lax.psum(jnp.sum(loss_mask).astype(jnp.float32), ('dp', 'ctx'))  42 us
    all_to_all x1, waiting for transfers between devices, body(): lax.all_to_all(query_split, 'ctx', split_axis=1, concat_axis=0, tiled=True)  41.9 us
    all_to_all x1, waiting for transfers between devices, body(): lax.all_to_all(outputs, 'ctx', split_axis=0, concat_axis=1, tiled=True)  41.6 us
    dot_general x3, matrix products, gather_values(): jnp.einsum('hqk,ke->qhe', weights, value_tile, preferred_element_type=jnp...  18.6 us
    unnamed x42, local copies, waits for them, and re-layouts  14.3 us
  transfers between devices with their start and end apart: 13, of which 8 were waited for; matrix products, arithmetic and copies ran while one was open for 6% of the time, Pallas kernels for 0%

commit v1 on v0

v1 whole, which is shorter than its diff:
```python
import functools
import math

import jax
import jax.numpy as jnp
from jax import lax
from jax.experimental import pallas as pl
from jax.experimental.pallas import tpu as pltpu
from jax.sharding import PartitionSpec as P

KEY_VALUE_HEADS = 8
HEAD_SIZE = 128
SCALE = 1.0 / math.sqrt(HEAD_SIZE)
LOG2E = math.log2(math.e)
NT = (((1,), (1,)), ((), ()))
NN = (((1,), (0,)), ((), ()))


def mm(a, b, dims=NN):
    return lax.dot_general(a, b, dims, preferred_element_type=jnp.float32)


def pair_rows(block):
    return jnp.concatenate([block[:, :HEAD_SIZE], block[:, HEAD_SIZE:]], 0)


def head_group(me, slots, rows, group, q_of, g_of, k_of, v_of, put_out, put_dq, s_ref, w_ref, x_ref, dk_ref, dv_ref):
    width = 2 * rows
    k_t = jnp.concatenate([k_of(s).T for s in range(slots)], 1)
    v_t = jnp.concatenate([v_of(s).T for s in range(slots)], 1)
    key_at = lax.broadcasted_iota(jnp.int32, (rows, width), 0)
    row_at = lax.broadcasted_iota(jnp.int32, (rows, width), 1) % rows
    tri = key_at <= row_at
    for pair in range(group // 2):
        q = pair_rows(q_of(pair))
        g = pair_rows(g_of(pair))
        top = None
        for s in range(slots):
            scores = mm(k_of(s), q, NT)
            if s == 0:
                scores = jnp.where(tri, scores, -1e30)
            s_ref[s * rows:(s + 1) * rows] = scores
            peak = jnp.max(scores, axis=0, keepdims=True)
            if s > 0:
                peak = jnp.where(s <= me, peak, -1e30)
            top = peak if top is None else jnp.maximum(top, peak)
        top = top * (SCALE * LOG2E)
        mass = None
        for s in range(slots):
            at = top if s == 0 else jnp.where(s <= me, top, 1e30)
            e = jnp.exp2(s_ref[s * rows:(s + 1) * rows] * (SCALE * LOG2E) - at)
            s_ref[s * rows:(s + 1) * rows] = e
            part = jnp.sum(e, axis=0, keepdims=True)
            mass = part if mass is None else mass + part
        inv = 1.0 / mass
        for s in range(slots):
            p = s_ref[s * rows:(s + 1) * rows] * inv
            w_ref[s * rows:(s + 1) * rows] = p.astype(jnp.bfloat16)
            s_ref[s * rows:(s + 1) * rows] = p
        out_t = mm(v_t, w_ref[...])
        out = out_t.T.astype(jnp.bfloat16)
        put_out(pair, out)
        prod = out.astype(jnp.float32) * g.astype(jnp.float32)
        delta = jnp.sum(prod.T, axis=0, keepdims=True)
        for s in range(slots):
            dots = mm(v_of(s), g, NT)
            x = (s_ref[s * rows:(s + 1) * rows] * (dots - delta)).astype(jnp.bfloat16)
            x_ref[s * rows:(s + 1) * rows] = x
        dv = mm(w_ref[...], g)
        dk = mm(x_ref[...], q)
        if pair == 0:
            dv_ref[...] = dv
            dk_ref[...] = dk
        else:
            dv_ref[...] += dv
            dk_ref[...] += dk
        put_dq(pair, mm(k_t, x_ref[...]).T)


def unpair(block, rows):
    return jnp.concatenate([block[:rows], block[rows:]], 1)


def compute_kernel(slots, rows, group, q_ref, g_ref, k_ref, v_ref, weight_ref, out_ref, dq_ref, dk_ref, dv_ref, s_ref, w_ref, x_ref, dk_acc, dv_acc):
    me = lax.axis_index("ctx")
    two = 2 * HEAD_SIZE

    def place(s):
        return pl.ds(pl.multiple_of(lax.rem(me + (slots - s), slots) * rows, rows), rows)

    def put_out(pair, out):
        out_ref[:, pair * two:(pair + 1) * two] = unpair(out, rows)

    def put_dq(pair, dq):
        dq_ref[:, pair * two:(pair + 1) * two] = unpair(dq * SCALE, rows).astype(jnp.bfloat16)

    head_group(
        me, slots, rows, group,
        lambda pair: q_ref[:, pair * two:(pair + 1) * two],
        lambda pair: (g_ref[:, pair * two:(pair + 1) * two].astype(jnp.float32) * weight_ref[...]).astype(jnp.bfloat16),
        lambda s: k_ref[place(s)],
        lambda s: v_ref[place(s)],
        put_out, put_dq, s_ref, w_ref, x_ref, dk_acc, dv_acc,
    )
    for s in range(slots):
        dk_ref[place(s)] = dk_acc[s * rows:(s + 1) * rows] * SCALE
        dv_ref[place(s)] = dv_acc[s * rows:(s + 1) * rows]


def body(query, key, value, out_grad, loss_mask):
    slots = lax.axis_size("ctx")
    rows = query.shape[1]
    group = query.shape[2] // key.shape[2]
    length = slots * rows
    all_tokens = query.shape[0] * length * lax.axis_size("dp")
    count = lax.psum(jnp.sum(loss_mask).astype(jnp.float32), ("dp", "ctx"))
    weight = (loss_mask[0].astype(jnp.float32) * (all_tokens / count))[:, None]
    kv = lax.all_gather(jnp.concatenate([key[0], value[0]], 1), "ctx", axis=0, tiled=False)
    kv = kv.reshape(length, -1)
    wide = group * HEAD_SIZE
    heads = KEY_VALUE_HEADS
    row_spec = pl.BlockSpec((rows, wide), lambda j: (0, j))
    key_spec = pl.BlockSpec((length, HEAD_SIZE), lambda j: (0, j))
    out, dq, dk, dv = pl.pallas_call(
        functools.partial(compute_kernel, slots, rows, group),
        grid=(heads,),
        in_specs=[
            row_spec, row_spec, key_spec,
            pl.BlockSpec((length, HEAD_SIZE), lambda j: (0, j + heads)),
            pl.BlockSpec((rows, 1), lambda j: (0, 0)),
        ],
        out_specs=[row_spec, row_spec, key_spec, key_spec],
        out_shape=[
            jax.ShapeDtypeStruct((rows, heads * wide), jnp.bfloat16),
            jax.ShapeDtypeStruct((rows, heads * wide), jnp.bfloat16),
            jax.ShapeDtypeStruct((length, heads * HEAD_SIZE), jnp.float32),
            jax.ShapeDtypeStruct((length, heads * HEAD_SIZE), jnp.float32),
        ],
        scratch_shapes=[
            pltpu.VMEM((length, 2 * rows), jnp.float32),
            pltpu.VMEM((length, 2 * rows), jnp.bfloat16),
            pltpu.VMEM((length, 2 * rows), jnp.bfloat16),
            pltpu.VMEM((length, HEAD_SIZE), jnp.float32),
            pltpu.VMEM((length, HEAD_SIZE), jnp.float32),
        ],
        compiler_params=pltpu.CompilerParams(vmem_limit_bytes=40 * 1024 * 1024),
    )(query[0], out_grad[0], kv, kv, weight)
    parts = jnp.concatenate([dk, dv], 1).reshape(slots, rows, -1)
    sums = lax.psum_scatter(parts, "ctx", scatter_dimension=0, tiled=False).astype(jnp.bfloat16)
    half = heads * HEAD_SIZE
    return (out[None], dq[None], sums[None, :, :half], sums[None, :, half:])


def solution(mesh):
    placed = P("dp", "ctx", None)
    return jax.shard_map(
        body,
        mesh=mesh,
        in_specs=(placed, placed, placed, placed, P("dp", "ctx")),
        out_specs=(placed, placed, placed, placed),
        check_vma=False,
    )
```

time: 663 us -> 300 us (0.45); the launches traced: 656 us -> 300 us
  waiting for transfers between devices: 375 us -> 180 us
  local copies, waits for them, and re-layouts: 93.9 us -> 4.12 us
  matrix products: 61.4 us -> 0 us
  Pallas kernels: 0 us -> 48.4 us
  starting transfers between devices: 35.6 us -> 0.08 us
  other arithmetic: 44 us -> 8.9 us
  between operations: 3.01 us -> 15.4 us
    ppermute x7 -> x0, waiting for transfers between devices: 271 us -> none  [swapped(): return lax.ppermute(block, axis, route)]
    reduce_scatter x0 -> x1, waiting for transfers between devices: none -> 147 us  [body(): lax.psum_scatter(parts, 'ctx', scatter_dimension=0, tiled=False)]
    all_to_all x6 -> x0, waiting for transfers between devices: 104 us -> none  [the longest x1 41.9 us: body(): lax.all_to_all(query_split, 'ctx', split_axis=1, concat_axis=0, tiled=True)]
    dot_general x21 -> x0, matrix products: 61.4 us -> none  [the longest x3 18.6 us: gather_values(): jnp.einsum('hqk,ke->qhe', weights, value_tile, preferred_element_type=jnp...]
    pallas_call x0 -> x1, Pallas kernels: none -> 48.4 us  [body(): pl.pallas_call(functools.partial(compute_kernel, slots, rows, group), gri...]
    all_gather x0 -> x1, waiting for transfers between devices: none -> 32.6 us  [body(): lax.all_gather(jnp.concatenate([key[0], value[0]], 1), 'ctx', axis=0, til...]
    all_to_all x6 -> x0, starting transfers between devices: 23.7 us -> none  [the longest x1 4.52 us: body(): lax.all_to_all(query_split, 'ctx', split_axis=1, concat_axis=0, tiled=True)]
    while x38 -> x0, local copies, waits for them, and re-layouts: 15.5 us -> none
  transfers between devices with their start and end apart: 13 -> 2, of which waited for: 8 -> 2; matrix products, arithmetic and copies ran while one was open for 6% -> 1% of each run, Pallas kernels for 0% -> 0%
where the time goes in v1:
time: 300 us
  waiting for transfers between devices  180 us (60%)
  Pallas kernels  48.4 us (16%)
  blocking collectives  43.3 us (14%)
  between operations  15.4 us (5%)
  other arithmetic  8.9 us (3%)
  local copies, waits for them, and re-layouts  4.12 us (1%)
    reduce_scatter x1, waiting for transfers between devices, body(): lax.psum_scatter(parts, 'ctx', scatter_dimension=0, tiled=False)  147 us
    pallas_call x1, Pallas kernels, body(): pl.pallas_call(functools.partial(compute_kernel, slots, rows, group), gri...  48.4 us
    psum x1, blocking collectives, body(): count = lax.psum(jnp.sum(loss_mask).astype(jnp.float32), ('dp', 'ctx'))  43.3 us
    all_gather x1, waiting for transfers between devices, body(): lax.all_gather(jnp.concatenate([key[0], value[0]], 1), 'ctx', axis=0, til...  32.6 us
  transfers between devices with their start and end apart: 2, of which 2 were waited for; matrix products, arithmetic and copies ran while one was open for 1% of the time, Pallas kernels for 0%

profile of v1, /device:TPU:0, one launch (start us, length us, event | category | flops | bytes accessed | tf_op | source)
XLA Modules:
  0.0 300.1 jit_solution(6638971658902170236)
XLA Ops:
  7.2 0.0 all-gather.3.cloned.1.call-start
  7.2 1.9 pad_maximum_fusion.1
  9.1 0.0 all-gather.3.cloned.1.call-update
  9.1 0.0 reduce-scatter.2.cloned.1.call-start
  9.2 1.3 reduce_sum.9
  11.1 43.3 %psum.7 = f32[]{:T(128)} all-reduce(f32[]{:T(128)S(6)} %convert_element_type.21), channel_id=1, replica_groups=mesh['dp'=4,'ctx'=8] {'dp','ctx'}, use_global_device_ids=true, to_apply=%region_1.0 | all-reduce | flops 1 | bytes 8 | tf_op jit(solution)/shard_map/psum | solution.py:116
  55.1 0.7 multiply_bitcast_fusion
  55.7 0.1 copy.9.weight_ref
  55.8 32.6 %all-gather.3.cloned.1.call-done.k_ref.v_ref = bf16[1024,2048]{1,0:T(8,128)(2,1)} async-done(((bf16[128,2048]{1,0:T(8,128)(2,1)}), bf16[1024,2048]{1,0:T(8,128)(2,1)}) %all-gather.3.cloned.1.call-update) | async-done | bytes 4194320 | tf_op jit(solution)/shard_map/all_gather | solution.py:118
  88.5 0.0 copy-start
  88.5 1.6 copy-done
  90.0 0.0 copy-start.1
  90.0 1.6 copy-done.1
  91.6 48.4 %shard_map.84 = (bf16[128,8192]{1,0:T(8,128)(2,1)}, bf16[128,8192]{1,0:T(8,128)(2,1)}, f32[1024,1024]{1,0:T(8,128)S(1)}, f32[1024,1024]{1,0:T(8,128)S(1)}) custom-call(bf16[128,8192]{1,0:T(8,128)(2,1)S(1)} %bitcast.15, bf16[128,8192]{1,0:T(8,128)(2,1)S(1)} %bitcast.16, bf16[1024,2048]{1,0:T(8,128)(2,1)} %all-gather.3.cloned.1.call-done.k_ref.v_ref, ...), custom_call_target="tpu_custom_call" | custom-call | tf_op jit(solution)/shard_map/pallas_call | solution.py:124
  140.1 3.8 %pad_maximum_fusion = f32[1024,2048]{1,0:T(8,128)} fusion(f32[1024,1024]{1,0:T(8,128)S(1)} %get-tuple-element.11, f32[1024,1024]{1,0:T(8,128)S(1)} %get-tuple-element.10), kind=kLoop, calls=%fused_computation | loop fusion | flops 2097152 | bytes 16777216 | tf_op jit(solution)/shard_map/concatenate | solution.py:148
  143.9 0.0 reduce-scatter.2.cloned.1.call-update
  143.9 147.3 %reduce-scatter.2.cloned.1.call-done = f32[1,128,2048]{2,1,0:T(8,128)} async-done(((f32[8,128,2048]{2,1,0:T(8,128)}), f32[1,128,2048]{2,1,0:T(8,128)}) %reduce-scatter.2.cloned.1.call-update) | async-done | bytes 1048592 | tf_op jit(solution)/shard_map/reduce_scatter | solution.py:149
  291.2 1.3 convert_bitcast_fusion
  292.5 0.8 slice_bitcast_fusion
Async XLA Ops:
  7.2 81.3 %all-gather.3.cloned.1.call-start = ((), (), s32[]{:S(2)}) async-start(), calls=%async_computation.2 | async-start | bytes 4718592 | tf_op jit(solution)/shard_map/all_gather | solution.py:118
  9.1 282.1 %reduce-scatter.2.cloned.1.call-start = ((), (), s32[]{:S(2)}) async-start(), calls=%async_computation.1 | async-start | bytes 9437184 | tf_op jit(solution)/shard_map/reduce_scatter | solution.py:149
  88.5 1.6 copy-start
  90.0 1.6 copy-start.1
Sparse Core Ops, SparseCore 0:
  10.7 77.7 all-gather.2
  144.0 147.1 reduce-scatter.1

commit v2 on v1

--- a/solution.py
+++ b/solution.py
@@ -81,80 +81,228 @@
     return jnp.concatenate([block[:rows], block[rows:]], 1)
 
 
-def compute_kernel(slots, rows, group, q_ref, g_ref, k_ref, v_ref, weight_ref, out_ref, dq_ref, dk_ref, dv_ref, s_ref, w_ref, x_ref, dk_acc, dv_acc):
+def fused_kernel(
+    slots, lines, copies, rows, group, heads, all_tokens,
+    q_ref, g_ref, k_ref, v_ref, mask_ref, count_ref,
+    out_ref, dq_ref, kv_ref,
+    s_ref, w_ref, x_ref, dk_acc, dv_acc,
+    stash, own, y_out, y_in, z_out, z_in, ctx_counts, dp_out, dp_counts, factor_ref,
+    y_sent, y_got, z_sent, z_got, c_sent, c_got, d_sent, d_got,
+):
+    step = pl.program_id(0)
     me = lax.axis_index("ctx")
+    batch = lax.axis_index("dp")
+    depths = slots // lines
+    depth, line = me // lines, lax.rem(me, lines)
     two = 2 * HEAD_SIZE
+
+    def at_ctx(shift):
+        return {"ctx": lax.rem(me + shift, slots)}
+
+    def at_dp(shift):
+        return {"dp": lax.rem(batch + shift, copies)}
+
+    def count_copy(shift):
+        return pltpu.make_async_remote_copy(
+            src_ref=count_ref, dst_ref=ctx_counts.at[shift - 1],
+            send_sem=c_sent.at[shift - 1], recv_sem=c_got.at[shift - 1],
+            device_id=at_ctx(shift), device_id_type=pl.DeviceIdType.MESH)
+
+    def total_copy(shift):
+        return pltpu.make_async_remote_copy(
+            src_ref=dp_out, dst_ref=dp_counts.at[shift - 1],
+            send_sem=d_sent.at[shift - 1], recv_sem=d_got.at[shift - 1],
+            device_id=at_dp(shift), device_id_type=pl.DeviceIdType.MESH)
+
+    def y_copy(head, hop, back):
+        return pltpu.make_async_remote_copy(
+            src_ref=y_out.at[head, hop - 1, back], dst_ref=y_in.at[head, hop - 1, back],
+            send_sem=y_sent.at[head, hop - 1, back], recv_sem=y_got.at[head, hop - 1, back],
+            device_id={"ctx": depth * lines + lax.rem(line + hop, lines)},
+            device_id_type=pl.DeviceIdType.MESH)
+
+    def z_copy(head, back):
+        return pltpu.make_async_remote_copy(
+            src_ref=z_out.at[head, back - 1], dst_ref=z_in.at[head, back - 1],
+            send_sem=z_sent.at[head, back - 1], recv_sem=z_got.at[head, back - 1],
+            device_id={"ctx": lax.rem(me + slots - back * lines, slots)},
+            device_id_type=pl.DeviceIdType.MESH)
+
+    @pl.when(step == 0)
+    def _():
+        barrier = pltpu.get_barrier_semaphore()
+        for shift in range(1, slots):
+            pl.semaphore_signal(barrier, inc=1, device_id=at_ctx(shift), device_id_type=pl.DeviceIdType.MESH)
+        for shift in range(1, copies):
+            pl.semaphore_signal(barrier, inc=1, device_id=at_dp(shift), device_id_type=pl.DeviceIdType.MESH)
+        pl.semaphore_wait(barrier, slots + copies - 2)
+        for shift in range(1, slots):
+            count_copy(shift).start()
 
     def place(s):
         return pl.ds(pl.multiple_of(lax.rem(me + (slots - s), slots) * rows, rows), rows)
 
     def put_out(pair, out):
         out_ref[:, pair * two:(pair + 1) * two] = unpair(out, rows)
+        if pair == 0:
+            @pl.when(step == 0)
+            def _():
+                total = count_ref[...]
+                for shift in range(1, slots):
+                    count_copy(shift).wait()
+                    total = total + ctx_counts[shift - 1]
+                dp_out[...] = total
+                for shift in range(1, copies):
+                    total_copy(shift).start()
 
     def put_dq(pair, dq):
-        dq_ref[:, pair * two:(pair + 1) * two] = unpair(dq * SCALE, rows).astype(jnp.bfloat16)
-
+        if pair == 0:
+            @pl.when(step == 0)
+            def _():
+                total = dp_out[...]
+                for shift in range(1, copies):
+                    total_copy(shift).wait()
+                    total = total + dp_counts[shift - 1]
+                factor_ref[...] = all_tokens / total
+        scaled = dq * SCALE * factor_ref[0:1, 0:1]
+        dq_ref[:, pair * two:(pair + 1) * two] = unpair(scaled, rows).astype(jnp.bfloat16)
+
+    mask = mask_ref[...]
     head_group(
         me, slots, rows, group,
         lambda pair: q_ref[:, pair * two:(pair + 1) * two],
-        lambda pair: (g_ref[:, pair * two:(pair + 1) * two].astype(jnp.float32) * weight_ref[...]).astype(jnp.bfloat16),
+        lambda pair: (g_ref[:, pair * two:(pair + 1) * two].astype(jnp.float32) * mask).astype(jnp.bfloat16),
         lambda s: k_ref[place(s)],
         lambda s: v_ref[place(s)],
         put_out, put_dq, s_ref, w_ref, x_ref, dk_acc, dv_acc,
     )
-    for s in range(slots):
-        dk_ref[place(s)] = dk_acc[s * rows:(s + 1) * rows] * SCALE
-        dv_ref[place(s)] = dv_acc[s * rows:(s + 1) * rows]
-
-
-def body(query, key, value, out_grad, loss_mask):
+
+    def partial_at(device):
+        s = lax.rem(me - device + slots, slots)
+        where = pl.ds(pl.multiple_of(s * rows, rows), rows)
+        return jnp.concatenate([dk_acc[where] * SCALE, dv_acc[where]], 1) * factor_ref[0:1, 0:1]
+
+    def send_across(head):
+        for back in range(depths):
+            @pl.when(back <= depth)
+            def _():
+                for hop in range(1, lines):
+                    other = (depth - back) * lines + lax.rem(line + hop, lines)
+                    y_out[head, hop - 1, back] = partial_at(other).astype(jnp.bfloat16)
+                    y_copy(head, hop, back).start()
+
+    def send_down(head):
+        for back in range(depths):
+            @pl.when(back <= depth)
+            def _():
+                total = stash[back]
+                for hop in range(1, lines):
+                    y_copy(head, hop, back).wait()
+                    total = total + y_in[head, hop - 1, back].astype(jnp.float32)
+                if back == 0:
+                    own[head] = total
+                else:
+                    z_out[head, back - 1] = total.astype(jnp.bfloat16)
+                    z_copy(head, back).start()
+
+    def keep():
+        for back in range(depths):
+            @pl.when(back <= depth)
+            def _():
+                stash[back] = partial_at(me - back * lines)
+
+    send_across(step)
+
+    @pl.when(step > 0)
+    def _():
+        send_down(step - 1)
+
+    keep()
+
+    @pl.when(step == heads - 1)
+    def _():
+        send_down(heads - 1)
+        for head in range(heads):
+            for back in range(1, depths):
+                @pl.when(depth + back < depths)
+                def _():
+                    z_copy(head, back).wait_recv()
+                    own[head] = own[head] + z_in[head, back - 1].astype(jnp.float32)
+
+                @pl.when(back <= depth)
+                def _():
+                    z_copy(head, back).wait_send()
+            total = own[head].astype(jnp.bfloat16)
+            kv_ref[:, head * HEAD_SIZE:(head + 1) * HEAD_SIZE] = total[:, :HEAD_SIZE]
+            kv_ref[:, (heads + head) * HEAD_SIZE:(heads + head + 1) * HEAD_SIZE] = total[:, HEAD_SIZE:]
+
+
+def body(lines, query, key, value, out_grad, loss_mask):
     slots = lax.axis_size("ctx")
+    copies = lax.axis_size("dp")
+    depths = slots // lines
     rows = query.shape[1]
     group = query.shape[2] // key.shape[2]
     length = slots * rows
-    all_tokens = query.shape[0] * length * lax.axis_size("dp")
-    count = lax.psum(jnp.sum(loss_mask).astype(jnp.float32), ("dp", "ctx"))
-    weight = (loss_mask[0].astype(jnp.float32) * (all_tokens / count))[:, None]
-    kv = lax.all_gather(jnp.concatenate([key[0], value[0]], 1), "ctx", axis=0, tiled=False)
-    kv = kv.reshape(length, -1)
+    all_tokens = float(query.shape[0] * length * copies)
+    mask = loss_mask[0].astype(jnp.float32)
+    count = jnp.broadcast_to(jnp.sum(mask), (8, HEAD_SIZE))
+    kv = lax.all_gather(jnp.concatenate([key[0], value[0]], 1), "ctx", axis=0, tiled=True)
     wide = group * HEAD_SIZE
     heads = KEY_VALUE_HEADS
+    two = 2 * HEAD_SIZE
     row_spec = pl.BlockSpec((rows, wide), lambda j: (0, j))
-    key_spec = pl.BlockSpec((length, HEAD_SIZE), lambda j: (0, j))
-    out, dq, dk, dv = pl.pallas_call(
-        functools.partial(compute_kernel, slots, rows, group),
+    whole = pl.BlockSpec(memory_space=pltpu.VMEM)
+    wait = pltpu.SemaphoreType.DMA
+    f32, b16 = jnp.float32, jnp.bfloat16
+    out, dq, grads = pl.pallas_call(
+        functools.partial(fused_kernel, slots, lines, copies, rows, group, heads, all_tokens),
         grid=(heads,),
         in_specs=[
-            row_spec, row_spec, key_spec,
+            row_spec, row_spec,
+            pl.BlockSpec((length, HEAD_SIZE), lambda j: (0, j)),
             pl.BlockSpec((length, HEAD_SIZE), lambda j: (0, j + heads)),
-            pl.BlockSpec((rows, 1), lambda j: (0, 0)),
+            whole, whole,
         ],
-        out_specs=[row_spec, row_spec, key_spec, key_spec],
+        out_specs=[row_spec, row_spec, whole],
         out_shape=[
-            jax.ShapeDtypeStruct((rows, heads * wide), jnp.bfloat16),
-            jax.ShapeDtypeStruct((rows, heads * wide), jnp.bfloat16),
-            jax.ShapeDtypeStruct((length, heads * HEAD_SIZE), jnp.float32),
-            jax.ShapeDtypeStruct((length, heads * HEAD_SIZE), jnp.float32),
+            jax.ShapeDtypeStruct((rows, heads * wide), b16),
+            jax.ShapeDtypeStruct((rows, heads * wide), b16),
+            jax.ShapeDtypeStruct((rows, heads * two), b16),
         ],
         scratch_shapes=[
-            pltpu.VMEM((length, 2 * rows), jnp.float32),
-            pltpu.VMEM((length, 2 * rows), jnp.bfloat16),
-            pltpu.VMEM((length, 2 * rows), jnp.bfloat16),
-            pltpu.VMEM((length, HEAD_SIZE), jnp.float32),
-            pltpu.VMEM((length, HEAD_SIZE), jnp.float32),
+            pltpu.VMEM((length, 2 * rows), f32),
+            pltpu.VMEM((length, 2 * rows), b16),
+            pltpu.VMEM((length, 2 * rows), b16),
+            pltpu.VMEM((length, HEAD_SIZE), f32),
+            pltpu.VMEM((length, HEAD_SIZE), f32),
+            pltpu.VMEM((depths, rows, two), f32),
+            pltpu.VMEM((heads, rows, two), f32),
+            pltpu.VMEM((heads, lines - 1, depths, rows, two), b16),
+            pltpu.VMEM((heads, lines - 1, depths, rows, two), b16),
+            pltpu.VMEM((heads, depths - 1, rows, two), b16),
+            pltpu.VMEM((heads, depths - 1, rows, two), b16),
+            pltpu.VMEM((slots - 1, 8, HEAD_SIZE), f32),
+            pltpu.VMEM((8, HEAD_SIZE), f32),
+            pltpu.VMEM((copies - 1, 8, HEAD_SIZE), f32),
+            pltpu.VMEM((8, HEAD_SIZE), f32),
+            wait((heads, lines - 1, depths)), wait((heads, lines - 1, depths)),
+            wait((heads, depths - 1)), wait((heads, depths - 1)),
+            wait((slots - 1,)), wait((slots - 1,)),
+            wait((copies - 1,)), wait((copies - 1,)),
         ],
-        compiler_params=pltpu.CompilerParams(vmem_limit_bytes=40 * 1024 * 1024),
-    )(query[0], out_grad[0], kv, kv, weight)
-    parts = jnp.concatenate([dk, dv], 1).reshape(slots, rows, -1)
-    sums = lax.psum_scatter(parts, "ctx", scatter_dimension=0, tiled=False).astype(jnp.bfloat16)
+        compiler_params=pltpu.CompilerParams(
+            vmem_limit_bytes=48 * 1024 * 1024, collective_id=0, has_side_effects=True),
+    )(query[0], out_grad[0], kv, kv, mask[:, None], count)
     half = heads * HEAD_SIZE
-    return (out[None], dq[None], sums[None, :, :half], sums[None, :, half:])
+    return (out[None], dq[None], grads[None, :, :half], grads[None, :, half:])
 
 
 def solution(mesh):
     placed = P("dp", "ctx", None)
+    lines = 2 if mesh.shape["ctx"] < 16 else 4
     return jax.shard_map(
-        body,
+        functools.partial(body, lines),
         mesh=mesh,
         in_specs=(placed, placed, placed, placed, P("dp", "ctx")),
         out_specs=(placed, placed, placed, placed),

time: 300 us -> 174 us (0.58)
  waiting for transfers between devices: 180 us -> 75.7 us
  blocking collectives: 43.3 us -> 0 us
  Pallas kernels: 48.4 us -> 76 us
  other arithmetic: 8.9 us -> 3.79 us
    reduce_scatter x1 -> x0, waiting for transfers between devices: 147 us -> none  [body(): lax.psum_scatter(parts, 'ctx', scatter_dimension=0, tiled=False)]
    psum x1 -> x0, blocking collectives: 43.3 us -> none  [body(): count = lax.psum(jnp.sum(loss_mask).astype(jnp.float32), ('dp', 'ctx'))]
    all_gather x1, waiting for transfers between devices: 32.6 us -> 75.7 us  [body(): lax.all_gather(jnp.concatenate([key[0], value[0]], 1), 'ctx', axis=0, til...]
    pallas_call x1, Pallas kernels: 48.4 us -> 76 us  [body(): pl.pallas_call(functools.partial(fused_kernel, slots, lines, copies, rows...]
    concatenate x1 -> x0, other arithmetic: 3.79 us -> none  [body(): parts = jnp.concatenate([dk, dv], 1).reshape(slots, rows, -1)]
  transfers between devices with their start and end apart: 2 -> 1, of which waited for: 2 -> 1; matrix products, arithmetic and copies ran while one was open for 1% -> 1% of each run, Pallas kernels for 0% -> 0%
where the time goes in v2:
time: 174 us
  Pallas kernels  76 us (44%)
  waiting for transfers between devices  75.7 us (44%)
  between operations  14 us (8%)
  local copies, waits for them, and re-layouts  4.22 us (2%)
  other arithmetic  3.79 us (2%)
    pallas_call x1, Pallas kernels, body(): pl.pallas_call(functools.partial(fused_kernel, slots, lines, copies, rows...  76 us
    all_gather x1, waiting for transfers between devices, body(): lax.all_gather(jnp.concatenate([key[0], value[0]], 1), 'ctx', axis=0, til...  75.7 us
  transfers between devices with their start and end apart: 1, of which 1 were waited for; matrix products, arithmetic and copies ran while one was open for 1% of the time, Pallas kernels for 0%

profile of v2, /device:TPU:0, one launch (start us, length us, event | category | flops | bytes accessed | tf_op | source)
XLA Modules:
  0.0 173.8 jit_solution(6147150006121691558)
XLA Ops:
  7.2 0.0 all-gather.2.cloned.1.call-start
  7.2 1.9 %pad_maximum_fusion = bf16[128,2048]{1,0:T(8,128)(2,1)} fusion(bf16[128,1024]{1,0:T(8,128)(2,1)} %bitcast.16, bf16[128,1024]{1,0:T(8,128)(2,1)} %bitcast.17), kind=kLoop, calls=%fused_computation | loop fusion | flops 1048576 | bytes 1048576 | tf_op jit(solution)/shard_map/concatenate | solution.py:250
  9.1 0.0 all-gather.2.cloned.1.call-update
  9.1 0.7 convert_bitcast_fusion
  9.8 0.1 copy.9.mask_ref
  9.9 1.3 convert_reduce_fusion
  11.1 75.7 %all-gather.2.cloned.1.call-done.k_ref.v_ref = bf16[1024,2048]{1,0:T(8,128)(2,1)} async-done(((bf16[128,2048]{1,0:T(8,128)(2,1)}), bf16[1024,2048]{1,0:T(8,128)(2,1)}) %all-gather.2.cloned.1.call-update) | async-done | bytes 4194320 | tf_op jit(solution)/shard_map/all_gather | solution.py:250
  86.8 0.6 broadcast_in_dim.16.count_ref
  87.5 76.0 %shard_map.84 = (bf16[128,8192]{1,0:T(8,128)(2,1)S(1)}, bf16[128,8192]{1,0:T(8,128)(2,1)S(1)}, bf16[128,2048]{1,0:T(8,128)(2,1)S(1)}) custom-call(bf16[128,8192]{1,0:T(8,128)(2,1)} %bitcast.14, bf16[128,8192]{1,0:T(8,128)(2,1)} %bitcast.15, bf16[1024,2048]{1,0:T(8,128)(2,1)} %all-gather.2.cloned.1.call-done.k_ref.v_ref, ...), custom_call_target="tpu_custom_call" | custom-call | tf_op jit(solution)/shard_map/pallas_call | solution.py:258
  163.5 0.8 slice_bitcast_fusion
  164.3 1.3 copy.12
  165.6 1.3 copy.13
Async XLA Ops:
  7.2 79.7 %all-gather.2.cloned.1.call-start = ((), (), s32[]{:S(2)}) async-start(), calls=%async_computation | async-start | bytes 4718592 | tf_op jit(solution)/shard_map/all_gather | solution.py:250
Sparse Core Ops, SparseCore 0:
  10.7 76.0 all-gather.1
